TPU v7x, 32 devices: a whole 2x2x4 slice. The times are simulated.
32 devices in a mesh: groups: 2 (over y), tp: 8 (over z, x), sq: 2 (over core).
Axes of the slice: x: 2, y: 2, z: 4, core: 2. Of those that a mesh axis runs over, the one named last changes fastest.
Arguments:
- hidden_states: bfloat16 [1024, 8192], P(('groups', 'sq'), 'tp'), parts along dimension 0, may hold values from -41 to 41
- out_grad: bfloat16 [1024, 8192], P(('groups', 'sq'), 'tp'), parts along dimension 0, may hold values from -6 to 6
- norm_gain: bfloat16 [8192], P('tp'), may hold values from 0.099609375 to 1.8984375
- w_gate: bfloat16 [8192, 16384], P('sq', 'tp'), may hold values from -0.0625 to 0.0625
- w_up: bfloat16 [8192, 16384], P('sq', 'tp'), may hold values from -0.0625 to 0.0625
- w_down: bfloat16 [16384, 8192], P('tp', 'sq'), may hold values from -0.046875 to 0.046875
- proj_model: bfloat16 [3, 8192, 64], P(None, 'tp'), may hold values from -0.0625 to 0.0625
- proj_hidden: bfloat16 [3, 16384, 64], P(None, 'tp'), may hold values from -0.046875 to 0.046875
- queries: bfloat16 [3, 256, 4096], P(None, ('tp', 'sq')), may hold values from -0.009765625 to 0.009765625
Outputs:
- scores: float32 [4, 256], P(('groups', 'sq'), 'tp'), parts along dimension 0
There are 2 independent parts, one for each index of `groups`. A program takes and returns all parts, laid end to end along the dimension named above; an argument that names none is the same for every part. Nothing has to cross between parts.
All inputs are finite; a program needn't handle non-finite values.
Results may differ from a plain program's by a relative error of at most 0.0052.
Values may be sent and summed in bfloat16 or wider, within the bound.
A program may use at most 320 MiB of HBM per device.

v0:
```python
import jax
import jax.numpy as jnp
from jax import lax
from jax.sharding import PartitionSpec as P

D = 8192
R = 64
SEQ_LEN = 256


EPS = 1e-05


def layer_features(columns, member):
    slot_pairs = ((3, 0), (4, 1), (2, 5))
    result = []
    for out_slot, in_slot in slot_pairs:
        outer = columns[:, out_slot * R : (out_slot + 1) * R]
        inner = columns[:, in_slot * R : (in_slot + 1) * R]
        block = jnp.einsum("te,to,ti->eoi", member, outer, inner, precision=lax.Precision.HIGHEST)
        result.append(block.reshape(member.shape[1], R * R))
    return jnp.stack(result, axis=1)


def membership(row_count, seq_count):
    token_seq = jnp.arange(row_count, dtype=jnp.int32) // SEQ_LEN
    return (token_seq[:, None] == jnp.arange(seq_count, dtype=jnp.int32)[None, :]).astype(
        jnp.float32
    )


def per_device(
    hidden_states, out_grad, norm_gain, w_gate, w_up, w_down, proj_model, proj_hidden, queries
):
    gate_full, up_full, down_full = (
        lax.all_gather(w_gate, "sq", axis=0, tiled=True),
        lax.all_gather(w_up, "sq", axis=0, tiled=True),
        lax.all_gather(w_down, "sq", axis=1, tiled=True),
    )
    row_count = hidden_states.shape[0]
    seq_count = row_count // SEQ_LEN
    states = hidden_states.astype(jnp.float32)
    row_total = lax.psum(jnp.sum(states * states, axis=1), "tp")
    factor = lax.rsqrt(row_total / D + EPS)
    normed = (states * factor[:, None] * norm_gain.astype(jnp.float32)).astype(jnp.bfloat16)
    shard_piece = lax.all_gather(normed, "tp", axis=1, tiled=True)
    gate = jnp.dot(shard_piece, gate_full, preferred_element_type=jnp.float32)
    upward = jnp.dot(shard_piece, up_full, preferred_element_type=jnp.float32)
    grad_act = lax.dot_general(
        lax.all_gather(out_grad, "tp", axis=1, tiled=True),
        down_full,
        (((1,), (1,)), ((), ())),
        preferred_element_type=jnp.float32,
    )
    sigmoid_gate = jax.nn.sigmoid(gate)
    swish = gate * sigmoid_gate
    activation = (swish * upward).astype(jnp.bfloat16)
    grad_gate = (grad_act * upward * sigmoid_gate * (1.0 + gate * (1.0 - sigmoid_gate))).astype(
        jnp.bfloat16
    )
    grad_up = (grad_act * swish).astype(jnp.bfloat16)
    sources = (normed, normed, out_grad, grad_gate, grad_up, activation)
    tables = (
        proj_model[0],
        proj_model[1],
        proj_model[2],
        proj_hidden[0],
        proj_hidden[1],
        proj_hidden[2],
    )
    pieces = []
    for source, table in zip(sources, tables):
        pieces.append(jnp.dot(source, table, preferred_element_type=jnp.float32))
    columns = lax.psum(jnp.concatenate(pieces, axis=1), "tp")
    features = layer_features(columns, membership(row_count, seq_count))
    paired = lax.all_gather(queries, "sq", axis=1, tiled=True)
    scores = jnp.einsum(
        "elk,lqk->eq", features, paired.astype(jnp.float32), precision=lax.Precision.HIGHEST
    )
    return scores


def solution(mesh):
    placed = (
        P(("groups", "sq"), "tp"),
        P(("groups", "sq"), "tp"),
        P("tp"),
        P("sq", "tp"),
        P("sq", "tp"),
        P("tp", "sq"),
        P(None, "tp", None),
        P(None, "tp", None),
        P(None, ("tp", "sq"), None),
    )
    return jax.shard_map(
        per_device, mesh=mesh, in_specs=placed, out_specs=P(("groups", "sq"), "tp"), check_vma=False
    )
```

profile of v0, /device:TPU:24, one launch (start us, length us, event | category | flops | bytes accessed | tf_op | source)
XLA Modules:
  0.0 442.7 jit_solution(10415204259441790939)
XLA Ops:
  6.5 0.0 all-gather.10.cloned.1.call-start
  6.5 0.7 convert_element_type.21
  7.2 1.2 fusion.1
  8.4 16.8 %psum.14 = f32[256]{0:T(256)S(1)} all-reduce(f32[256]{0:T(256)S(1)} %fusion.1), channel_id=1, replica_groups=mesh['groups'=2,'tp'=8,'sq'=2] {'tp'}, use_global_device_ids=true, to_apply=%region_1.0 | all-reduce | flops 256 | bytes 2048 | tf_op jit(solution)/shard_map/psum | solution.py:43
  25.3 2.0 fusion.3
  27.3 0.0 all-gather.10.cloned.1.call-update
  27.3 0.0 all-gather.14.cloned.1.call-start
  27.4 0.7 all-gather.14.cloned.1.call-update
  28.1 0.0 all-gather.12.cloned.1.call-start
  28.1 0.7 all-gather.12.cloned.1.call-update
  28.8 0.0 all-gather.6.cloned.1.call-start
  28.9 0.5 all-gather.6.cloned.1.call-update
  29.4 0.0 copy-start
  29.4 0.0 copy-start.4
  29.4 0.0 copy-start.1
  29.4 0.0 all-gather.8.cloned.1.call-start
  29.5 0.5 all-gather.8.cloned.1.call-update
  30.0 0.0 all-reduce.2.cloned.1.call-start
  30.1 0.4 copy-done
  30.4 0.1 copy-done.4
  30.6 0.3 convolution_dynamic-update-slice_fusion.5
  30.8 0.3 convolution_dynamic-update-slice_fusion.4
  31.1 0.0 copy-done.1
  31.1 0.3 convolution_dynamic-update-slice_fusion.3
  31.4 69.5 %all-gather.10.cloned.1.call-done = bf16[256,8192]{1,0:T(8,128)(2,1)} async-done(((bf16[256,1024]{1,0:T(8,128)(2,1)}), bf16[256,8192]{1,0:T(8,128)(2,1)}) %all-gather.10.cloned.1.call-update) | async-done | bytes 4194320 | tf_op jit(solution)/shard_map/all_gather | solution.py:46
  101.0 53.1 %all-gather.14.cloned.1.call-done = bf16[8192,2048]{1,0:T(8,128)(2,1)} async-done(((bf16[4096,2048]{1,0:T(8,128)(2,1)}), bf16[8192,2048]{1,0:T(8,128)(2,1)}) %all-gather.14.cloned.1.call-update) | async-done | bytes 33554448 | tf_op jit(solution)/shard_map/all_gather | solution.py:36
  154.1 20.7 %fusion.33 = f32[256,2048]{1,0:T(8,128)} fusion(bf16[256,8192]{1,0:T(8,128)(2,1)} %all-gather.10.cloned.1.call-done, bf16[8192,2048]{1,0:T(8,128)(2,1)} %all-gather.14.cloned.1.call-done), kind=kOutput, calls=%fused_computation.54 | convolution fusion | flops 8589934592 | bytes 39845888 | tf_op jit(solution)/shard_map/dot_general | solution.py:47
  174.7 33.3 %all-gather.12.cloned.1.call-done = bf16[8192,2048]{1,0:T(8,128)(2,1)} async-done(((bf16[4096,2048]{1,0:T(8,128)(2,1)}), bf16[8192,2048]{1,0:T(8,128)(2,1)}) %all-gather.12.cloned.1.call-update) | async-done | bytes 33554448 | tf_op jit(solution)/shard_map/all_gather | solution.py:37
  208.1 17.6 %fusion.32 = f32[256,2048]{1,0:T(8,128)} fusion(bf16[256,8192]{1,0:T(8,128)(2,1)} %all-gather.10.cloned.1.call-done, bf16[8192,2048]{1,0:T(8,128)(2,1)} %all-gather.12.cloned.1.call-done), kind=kOutput, calls=%fused_computation.53 | convolution fusion | flops 8589934592 | bytes 39845888 | tf_op jit(solution)/shard_map/dot_general | solution.py:48
  225.7 57.0 %all-gather.6.cloned.1.call-done = bf16[256,8192]{1,0:T(8,128)(2,1)} async-done(((bf16[256,1024]{1,0:T(8,128)(2,1)}), bf16[256,8192]{1,0:T(8,128)(2,1)}) %all-gather.6.cloned.1.call-update) | async-done | bytes 4194320 | tf_op jit(solution)/shard_map/all_gather | solution.py:50
  282.7 53.0 %all-gather.8.cloned.1.call-done = bf16[2048,8192]{1,0:T(8,128)(2,1)} async-done(((bf16[2048,4096]{1,0:T(8,128)(2,1)}), bf16[2048,8192]{1,0:T(8,128)(2,1)}) %all-gather.8.cloned.1.call-update) | async-done | bytes 33554448 | tf_op jit(solution)/shard_map/all_gather | solution.py:38
  335.6 16.9 %fusion.31 = f32[256,2048]{1,0:T(8,128)} fusion(bf16[256,8192]{1,0:T(8,128)(2,1)} %all-gather.6.cloned.1.call-done, bf16[2048,8192]{1,0:T(8,128)(2,1)} %all-gather.8.cloned.1.call-done), kind=kOutput, calls=%fused_computation.52 | convolution fusion | flops 8589934592 | bytes 39845888 | tf_op jit(solution)/shard_map/dot_general | solution.py:49
  352.5 3.9 convolution_dynamic-update-slice_fusion.2
  356.4 0.1 copy-done.8
  356.6 0.7 convolution_dynamic-update-slice_fusion.1
  357.3 0.9 copy-done.7
  358.2 0.7 convolution_dynamic-update-slice_fusion
  358.9 0.7 copy-done.2
  359.6 0.0 all-reduce.2.cloned.1.call-update
  359.7 2.4 all_gather.23
  362.1 68.9 %all-reduce.2.cloned.1.call-done = f32[256,384]{0,1:T(8,128)} async-done(((f32[256,384]{0,1:T(8,128)}), f32[256,384]{0,1:T(8,128)}) %all-reduce.2.cloned.1.call-update) | async-done | bytes 393232 | tf_op jit(solution)/shard_map/psum | solution.py:74
  431.0 1.1 fusion.22
  432.1 0.1 transpose.11
  432.2 1.1 fusion.20
  433.2 0.1 transpose.12
  433.3 1.1 fusion.18
  434.4 0.1 transpose.13
  434.6 1.3 convolution_bitcast_fusion
  (12 shorter events, 0.1 us)
Async XLA Ops:
  6.5 94.4 %all-gather.10.cloned.1.call-start = ((), (), s32[]{:S(2)}) async-start(), calls=%async_computation.2 | async-start | bytes 4718592 | tf_op jit(solution)/shard_map/all_gather | solution.py:46
  27.3 126.7 %all-gather.14.cloned.1.call-start = ((), (), s32[]{:S(2)}) async-start(), calls=%async_computation.4 | async-start | bytes 50331648 | tf_op jit(solution)/shard_map/all_gather | solution.py:36
  28.1 180.0 %all-gather.12.cloned.1.call-start = ((), (), s32[]{:S(2)}) async-start(), calls=%async_computation.3 | async-start | bytes 50331648 | tf_op jit(solution)/shard_map/all_gather | solution.py:37
  28.8 253.8 %all-gather.6.cloned.1.call-start = ((), (), s32[]{:S(2)}) async-start(), calls=%async_computation | async-start | bytes 4718592 | tf_op jit(solution)/shard_map/all_gather | solution.py:50
  29.4 1.0 copy-start
  29.4 1.1 copy-start.4
  29.4 1.7 copy-start.1
  29.4 306.2 %all-gather.8.cloned.1.call-start = ((), (), s32[]{:S(2)}) async-start(), calls=%async_computation.1 | async-start | bytes 50331648 | tf_op jit(solution)/shard_map/all_gather | solution.py:38
  30.0 401.0 %all-reduce.2.cloned.1.call-start = ((), (), s32[]{:S(2)}) async-start(), calls=%async_computation.5 | async-start | bytes 786432 | tf_op jit(solution)/shard_map/psum | solution.py:74
  225.7 126.8 %copy-start.5 = (bf16[3,2048,64]{1,2,0:T(8,128)(2,1)S(1)}, bf16[3,2048,64]{1,2,0:T(8,128)(2,1)}, u32[]{:S(2)}) copy-start(bf16[3,2048,64]{1,2,0:T(8,128)(2,1)} %param.16) | copy-start | bytes 2359300
  352.5 4.0 copy-start.6
  352.5 4.1 copy-start.8
  356.6 1.6 copy-start.7
  358.2 1.5 copy-start.3
  358.9 0.7 copy-start.2
Sparse Core Ops, SparseCore 0:
  27.5 73.4 all-gather.9
  102.5 51.5 all-gather.13
  155.6 52.3 all-gather.11
  210.1 72.5 all-gather.5
  284.1 51.5 all-gather.7
  359.8 71.1 all-reduce.1
where the time goes:
time: 446 us; the launch traced here: 443 us
  waiting for transfers between devices  337 us (76%)
  matrix products  65.9 us (15%)
  blocking collectives  19.2 us (4%)
  between operations  13.6 us (3%)
    all_gather x1, waiting for transfers between devices, per_device(): shard_piece = lax.all_gather(normed, 'tp', axis=1, tiled=True)  69.5 us
    psum x1, waiting for transfers between devices, per_device(): columns = lax.psum(jnp.concatenate(pieces, axis=1), 'tp')  68.9 us
    all_gather x1, waiting for transfers between devices, per_device(): lax.all_gather(out_grad, 'tp', axis=1, tiled=True)  57 us
    all_gather x1, waiting for transfers between devices, per_device(): lax.all_gather(w_gate, 'sq', axis=0, tiled=True)  53.1 us
    all_gather x1, waiting for transfers between devices, per_device(): lax.all_gather(w_down, 'sq', axis=1, tiled=True)  53 us
    all_gather x1, waiting for transfers between devices, per_device(): lax.all_gather(w_up, 'sq', axis=0, tiled=True)  33.3 us
    dot_general x1, matrix products, per_device(): gate = jnp.dot(shard_piece, gate_full, preferred_element_type=jnp.float32)  20.7 us
    dot_general x1, matrix products, per_device(): upward = jnp.dot(shard_piece, up_full, preferred_element_type=jnp.float32)  17.6 us
  transfers between devices with their start and end apart: 6, of which 6 were waited for; matrix products, arithmetic and copies ran while one was open for 9% of the time, Pallas kernels for 0%

commit v1 on v0

v1 whole, which is shorter than its diff:
```python
import functools

import jax
import jax.numpy as jnp
from jax import lax
from jax.experimental import pallas as pl
from jax.experimental.pallas import tpu as pltpu
from jax.sharding import PartitionSpec as P

D = 8192
R = 64
SEQ_LEN = 256
EPS = 1e-05
NB = 2
NC = 4
MESH = pl.DeviceIdType.MESH
HIGH = lax.Precision.HIGHEST
ARRIVALS = (
    (0, 2, 4, 6),
    (0, 1, 2, 4),
    (0, 1, 2, 3),
    (0, 1, 3, 5),
    (1, 3, 5, 7),
    (3, 5, 6, 7),
    (4, 5, 6, 7),
    (2, 4, 6, 7),
)


def dot(a, b, dims=((1,), (0,)), precision=None):
    return lax.dot_general(a, b, (dims, ((), ())), precision=precision, preferred_element_type=jnp.float32)


def kernel(
    hid_ref, og_ref, gain_ref, wg_ref, wu_ref, wd_ref, pm_ref, ph_ref, q_ref, out_ref,
    hid, og, nm, pm, ph, qb, rs, grid_in, wdb, wgb, wub, acc_a, acc_gu, rec_a, rec_gu, cols, cols_in, feat, feat_in,
    load_sem, w_sem, g_recv, own_send, core_send, relay_send, rs_send, rs_recv, q_send, q_recv,
    pa_send, pa_recv, px_send, px_recv, c_send, c_recv, f_send, f_recv,
):
    t = lax.axis_index("tp")
    s = lax.axis_index("sq")
    o = 1 - s
    rows, width = hid.shape
    bt = rows // NB
    hl = acc_a.shape[1]
    nc = hl // NC
    share = bt // 8

    def t_of(p):
        return jnp.where(p < 4, 2 * p, 15 - 2 * p)

    zz = t // 2
    pos = jnp.where(t % 2 == 0, zz, 7 - zz)
    right = t_of((pos + 1) % 8)
    left = t_of((pos + 7) % 8)
    place = (pos + 2 + 4 * s) % 8
    half = t // 4
    slot = t % 4

    def remote(src, dst, send, recv, dev):
        return pltpu.make_async_remote_copy(
            src_ref=src, dst_ref=dst, send_sem=send, recv_sem=recv, device_id=dev, device_id_type=MESH
        )

    loads = [
        pltpu.make_async_copy(hid_ref, hid, load_sem.at[0]),
        pltpu.make_async_copy(og_ref, og, load_sem.at[1]),
        pltpu.make_async_copy(pm_ref, pm, load_sem.at[2]),
        pltpu.make_async_copy(ph_ref, ph, load_sem.at[3]),
        pltpu.make_async_copy(q_ref, qb.at[s], load_sem.at[4]),
    ]
    for c in loads:
        c.start()

    steps = []
    for i in range(4):
        j = jnp.int32(0)
        for c in range(8):
            j = j + jnp.where(place == c, ARRIVALS[c][i], 0)
        dist = (j + 1) // 2
        odd = j % 2
        src_pos = (pos + 8 + dist * (1 - 2 * odd)) % 8
        src_slot = t_of(src_pos) % 4
        target = jnp.where(odd == 1, right, left)
        passes = [
            (j >= 1) & (dist < jnp.where(odd == 1, 4, 3)),
            (j >= 1) & (dist < jnp.where(odd == 1, 3, 4)),
        ]
        steps.append((src_slot, target, passes))

    def w_load(a, i):
        at = steps[i][0] * width
        at = pl.multiple_of(at, width)
        if a == 0:
            return [pltpu.make_async_copy(wd_ref.at[:, pl.ds(at, width)], wdb.at[i % 2], w_sem.at[0, i % 2])]
        return [
            pltpu.make_async_copy(wg_ref.at[pl.ds(at, width), :], wgb.at[i % 2], w_sem.at[1, i % 2]),
            pltpu.make_async_copy(wu_ref.at[pl.ds(at, width), :], wub.at[i % 2], w_sem.at[2, i % 2]),
        ]

    for a in range(2):
        for i in range(2):
            for c in w_load(a, i):
                c.start()

    barrier = pltpu.get_barrier_semaphore()
    for d in range(1, 8):
        pl.semaphore_signal(barrier, inc=1, device_id={"tp": (t + d) % 8}, device_id_type=MESH)
    for tt in (t, left, right):
        pl.semaphore_signal(barrier, inc=1, device_id={"tp": tt, "sq": o}, device_id_type=MESH)
    pl.semaphore_wait(barrier, 10)

    def own_copies(a, b):
        at = pl.ds(pl.multiple_of(b * bt, bt), bt)
        src = og_ref.at[at, :] if a == 0 else nm.at[at, :]
        dst = grid_in.at[a, b, slot, s]
        recv = g_recv.at[a, b, slot, s]
        away = [
            remote(src, dst, own_send.at[a, b, 0], recv, {"tp": right, "sq": half}),
            remote(src, dst, own_send.at[a, b, 1], recv, {"tp": left, "sq": half}),
        ]
        core = remote(src, dst, core_send.at[a, b], recv, {"sq": o})
        here = pltpu.make_async_copy(src, dst, recv)
        return away, core, here

    def own_start(a, b):
        away, core, here = own_copies(a, b)
        for c in away:
            c.start()

        @pl.when(half != s)
        def _():
            core.start()

        @pl.when(half == s)
        def _():
            here.start()

    own_start(0, 0)
    q_copy = remote(q_ref, qb.at[s], q_send, q_recv, {"sq": o})
    q_copy.start()

    loads[0].wait()
    states = hid[...].astype(jnp.float32)
    sums = jnp.sum(states * states, axis=1, keepdims=True)
    rs[0] = jnp.transpose(jnp.broadcast_to(sums, (rows, 128)))[0:8]
    rs_copies = [
        remote(rs.at[0], rs.at[d], rs_send.at[d], rs_recv.at[d], {"tp": (t + d) % 8}) for d in range(1, 8)
    ]
    for c in rs_copies:
        c.start()
    loads[1].wait()
    loads[2].wait()
    c2 = dot(og[...], pm[2])
    for c in rs_copies:
        c.wait_recv()
    total = rs[0]
    for d in range(1, 8):
        total = total + rs[d]
    factor = lax.rsqrt(total / D + EPS)
    factor = jnp.transpose(jnp.broadcast_to(factor[0:1], (128, rows)))[:, 0:1]
    nm[...] = (hid[...].astype(jnp.float32) * factor * gain_ref[...].astype(jnp.float32)).astype(jnp.bfloat16)
    own_start(1, 0)
    c0 = dot(nm[...], pm[0])
    c1 = dot(nm[...], pm[1])
    for b in range(NB):
        part = slice(b * bt, (b + 1) * bt)
        cols[b, :, 0:128] = jnp.concatenate([c0[part], c1[part]], axis=1)
        cols[b, :, 128:256] = jnp.concatenate([c2[part], c2[part]], axis=1)
    loads[3].wait()

    def relays(a, b, i, k):
        src_slot, target, passes = steps[i]
        chunk = grid_in.at[a, b, src_slot, k]
        copy = remote(
            chunk, chunk, relay_send.at[a, b, i, k], g_recv.at[a, b, src_slot, k], {"tp": target}
        )
        return copy, passes[k]

    def arrive(a, b, i):
        for k in range(2):
            copy, passing = relays(a, b, i, k)
            copy.wait_recv()

            @pl.when(passing)
            def _():
                copy.start()

    def refill(a, b, i):
        if i < 2:
            for c in w_load(a, i + 2):
                c.start()
        else:

            @pl.when(b + 1 < NB)
            def _():
                for c in w_load(a, i - 2):
                    c.start()

    def pa_copy(b):
        return remote(
            acc_a.at[pl.ds(pl.multiple_of(o * bt, bt), bt), :], rec_a.at[b], pa_send.at[b], pa_recv.at[b], {"sq": o}
        )

    def px_copy(b, n):
        lanes = pl.ds(pl.multiple_of(n * nc, nc), nc)
        return remote(
            acc_gu.at[:, pl.ds(pl.multiple_of(o * bt, bt), bt), lanes],
            rec_gu.at[b, :, :, lanes],
            px_send.at[b, n],
            px_recv.at[b, n],
            {"sq": o},
        )

    def c_copy(b, d):
        peer = (t + d) % 8
        return remote(
            cols.at[b, pl.ds(pl.multiple_of(peer * share, share), share), :],
            cols_in.at[b, d],
            c_send.at[b, d],
            c_recv.at[b, d],
            {"tp": peer},
        )

    def block(b, carry):
        @pl.when(b + 1 < NB)
        def _():
            own_start(0, b + 1)

        for i in range(4):
            arrive(0, b, i)
            for c in w_load(0, i):
                c.wait()
            src_slot = steps[i][0]

            def down(n, carry):
                lanes = pl.ds(pl.multiple_of(n * nc, nc), nc)
                lhs = grid_in[0, b, src_slot].reshape(2 * bt, width)
                got = dot(lhs, wdb[i % 2, lanes, :], ((1,), (1,)))
                acc_a[:, lanes] = got if i == 0 else acc_a[:, lanes] + got
                return carry

            lax.fori_loop(0, NC, down, 0)
            refill(0, b, i)
        pa_copy(b).start()

        @pl.when(b + 1 < NB)
        def _():
            own_start(1, b + 1)

        for i in range(4):
            arrive(1, b, i)
            for c in w_load(1, i):
                c.wait()
            src_slot = steps[i][0]

            def gate_up(n, carry):
                lanes = pl.ds(pl.multiple_of(n * nc, nc), nc)
                lhs = grid_in[1, b, src_slot].reshape(2 * bt, width)
                for m, buf in ((0, wgb), (1, wub)):
                    got = dot(lhs, buf[i % 2, :, lanes])
                    acc_gu[m, :, lanes] = got if i == 0 else acc_gu[m, :, lanes] + got
                if i == 3:
                    px_copy(b, n).start()
                return carry

            lax.fori_loop(0, NC, gate_up, 0)
            refill(1, b, i)

        pa_copy(b).wait_recv()
        mine = pl.ds(pl.multiple_of(s * bt, bt), bt)

        def hidden(n, carry):
            px_copy(b, n).wait_recv()
            lanes = pl.ds(pl.multiple_of(n * nc, nc), nc)
            gate = acc_gu[0, mine, lanes] + rec_gu[b, 0, :, lanes]
            upward = acc_gu[1, mine, lanes] + rec_gu[b, 1, :, lanes]
            grad_act = acc_a[mine, lanes] + rec_a[b, :, lanes]
            sig = jax.nn.sigmoid(gate)
            swish = gate * sig
            activation = (swish * upward).astype(jnp.bfloat16)
            grad_gate = (grad_act * upward * sig * (1.0 + gate * (1.0 - sig))).astype(jnp.bfloat16)
            grad_up = (grad_act * swish).astype(jnp.bfloat16)
            return (
                carry[0] + dot(grad_gate, ph[0, lanes, :]),
                carry[1] + dot(grad_up, ph[1, lanes, :]),
                carry[2] + dot(activation, ph[2, lanes, :]),
            )

        zero = jnp.zeros((bt, R), jnp.float32)
        c3, c4, c5 = lax.fori_loop(0, NC, hidden, (zero, zero, zero))
        cols[b, :, 128:256] = jnp.concatenate([cols[b, :, 128:192], c3], axis=1)
        cols[b, :, 256:384] = jnp.concatenate([c4, c5], axis=1)
        for d in range(1, 8):
            c_copy(b, d).start()
        pa_copy(b).wait_send()
        for n in range(NC):
            px_copy(b, n).wait_send()
        return carry

    lax.fori_loop(0, NB, block, 0)

    tokens = []
    for b in range(NB):
        whole = cols[b, pl.ds(pl.multiple_of(t * share, share), share), :]
        for d in range(1, 8):
            c_copy(b, d).wait_recv()
            whole = whole + cols_in[b, d]
        tokens.append(whole)
    tokens = jnp.concatenate(tokens, axis=0)
    row = lax.broadcasted_iota(jnp.int32, (R, R), 0)
    col = lax.broadcasted_iota(jnp.int32, (R, R), 1)
    order = jnp.where(row < R // 2, 2 * row, 2 * row - R + 1)
    pick = (col == order).astype(jnp.float32)
    for layer, (out_slot, in_slot) in enumerate(((3, 0), (4, 1), (2, 5))):
        outer = tokens[:, out_slot * R : (out_slot + 1) * R]
        inner = tokens[:, in_slot * R : (in_slot + 1) * R]
        pair = dot(outer, inner, ((0,), (0,)), HIGH)
        pair = dot(pick, pair, precision=HIGH)
        feat[layer * 32 : (layer + 1) * 32] = jnp.concatenate([pair[0:32], pair[32:64]], axis=1)
    f_copies = [remote(feat, feat_in.at[d], f_send.at[d], f_recv.at[d], {"tp": (t + d) % 8}) for d in range(1, 8)]
    for c in f_copies:
        c.start()
    loads[4].wait()
    q_copy.wait_recv()
    whole = feat[...]
    for d in range(1, 8):
        f_copies[d - 1].wait_recv()
        whole = whole + feat_in[d]
    acc = jnp.zeros((2, 16, 128), jnp.float32)
    for layer in range(3):
        for j in range(32):
            line = whole[layer * 32 + j : layer * 32 + j + 1]
            acc = acc + qb[:, layer, :, j * 128 : (j + 1) * 128].astype(jnp.float32) * line[None]
    out_ref[...] = dot(jnp.ones((1, 128), jnp.float32), acc.reshape(32, 128), ((1,), (1,)), HIGH)

    q_copy.wait_send()
    for c in rs_copies + f_copies:
        c.wait_send()

    def drain(b, carry):
        for a in range(2):
            away, core, _ = own_copies(a, b)
            for c in away:
                c.wait_send()

            @pl.when(half != s)
            def _():
                core.wait_send()

            for i in range(4):
                for k in range(2):
                    copy, passing = relays(a, b, i, k)

                    @pl.when(passing)
                    def _():
                        copy.wait_send()

        for d in range(1, 8):
            c_copy(b, d).wait_send()
        return carry

    lax.fori_loop(0, NB, drain, 0)


def ring_device(hidden_states, out_grad, norm_gain, w_gate, w_up, w_down, proj_model, proj_hidden, queries):
    rows, width = hidden_states.shape
    hl = w_gate.shape[1]
    bt = rows // NB
    share = bt // 8
    bf, f32 = jnp.bfloat16, jnp.float32
    dma = pltpu.SemaphoreType.DMA
    anywhere = pl.BlockSpec(memory_space=pl.ANY)
    vmem = pl.BlockSpec(memory_space=pltpu.VMEM)
    return pl.pallas_call(
        kernel,
        out_shape=jax.ShapeDtypeStruct((1, 32), f32),
        in_specs=[anywhere, anywhere, vmem] + [anywhere] * 6,
        out_specs=vmem,
        scratch_shapes=[
            pltpu.VMEM((rows, width), bf),
            pltpu.VMEM((rows, width), bf),
            pltpu.VMEM((rows, width), bf),
            pltpu.VMEM(proj_model.shape, bf),
            pltpu.VMEM(proj_hidden.shape, bf),
            pltpu.VMEM((2,) + queries.shape, bf),
            pltpu.VMEM((8, 8, rows), f32),
            pltpu.VMEM((2, NB, 4, 2, bt, width), bf),
            pltpu.VMEM((2, hl, width), bf),
            pltpu.VMEM((2, width, hl), bf),
            pltpu.VMEM((2, width, hl), bf),
            pltpu.VMEM((2 * bt, hl), f32),
            pltpu.VMEM((2, 2 * bt, hl), f32),
            pltpu.VMEM((NB, bt, hl), f32),
            pltpu.VMEM((NB, 2, bt, hl), f32),
            pltpu.VMEM((NB, bt, 6 * R), f32),
            pltpu.VMEM((NB, 8, share, 6 * R), f32),
            pltpu.VMEM((96, 128), f32),
            pltpu.VMEM((8, 96, 128), f32),
            dma((5,)),
            dma((3, 2)),
            dma((2, NB, 4, 2)),
            dma((2, NB, 2)),
            dma((2, NB)),
            dma((2, NB, 4, 2)),
            dma((8,)),
            dma((8,)),
            dma,
            dma,
            dma((NB,)),
            dma((NB,)),
            dma((NB, NC)),
            dma((NB, NC)),
            dma((NB, 8)),
            dma((NB, 8)),
            dma((8,)),
            dma((8,)),
        ],
        compiler_params=pltpu.CompilerParams(
            collective_id=0, has_side_effects=True, vmem_limit_bytes=60 * 1024 * 1024
        ),
        cost_estimate=pl.CostEstimate(flops=26 * 10**9, bytes_accessed=10**8, transcendentals=10**6),
    )(
        hidden_states, out_grad, norm_gain.reshape(1, width), w_gate, w_up, w_down, proj_model, proj_hidden, queries
    )


def layer_features(columns, member):
    slot_pairs = ((3, 0), (4, 1), (2, 5))
    result = []
    for out_slot, in_slot in slot_pairs:
        outer = columns[:, out_slot * R : (out_slot + 1) * R]
        inner = columns[:, in_slot * R : (in_slot + 1) * R]
        block = jnp.einsum("te,to,ti->eoi", member, outer, inner, precision=HIGH)
        result.append(block.reshape(member.shape[1], R * R))
    return jnp.stack(result, axis=1)


def membership(row_count, seq_count):
    token_seq = jnp.arange(row_count, dtype=jnp.int32) // SEQ_LEN
    return (token_seq[:, None] == jnp.arange(seq_count, dtype=jnp.int32)[None, :]).astype(jnp.float32)


def wide_device(hidden_states, out_grad, norm_gain, w_gate, w_up, w_down, proj_model, proj_hidden, queries):
    gate_full, up_full, down_full = (
        lax.all_gather(w_gate, "sq", axis=0, tiled=True),
        lax.all_gather(w_up, "sq", axis=0, tiled=True),
        lax.all_gather(w_down, "sq", axis=1, tiled=True),
    )
    row_count = hidden_states.shape[0]
    seq_count = row_count // SEQ_LEN
    states = hidden_states.astype(jnp.float32)
    row_total = lax.psum(jnp.sum(states * states, axis=1), "tp")
    factor = lax.rsqrt(row_total / D + EPS)
    normed = (states * factor[:, None] * norm_gain.astype(jnp.float32)).astype(jnp.bfloat16)
    shard_piece = lax.all_gather(normed, "tp", axis=1, tiled=True)
    gate = jnp.dot(shard_piece, gate_full, preferred_element_type=jnp.float32)
    upward = jnp.dot(shard_piece, up_full, preferred_element_type=jnp.float32)
    grad_act = lax.dot_general(
        lax.all_gather(out_grad, "tp", axis=1, tiled=True),
        down_full,
        (((1,), (1,)), ((), ())),
        preferred_element_type=jnp.float32,
    )
    sigmoid_gate = jax.nn.sigmoid(gate)
    swish = gate * sigmoid_gate
    activation = (swish * upward).astype(jnp.bfloat16)
    grad_gate = (grad_act * upward * sigmoid_gate * (1.0 + gate * (1.0 - sigmoid_gate))).astype(jnp.bfloat16)
    grad_up = (grad_act * swish).astype(jnp.bfloat16)
    sources = (normed, normed, out_grad, grad_gate, grad_up, activation)
    pieces = []
    for i, source in enumerate(sources):
        table = proj_model[i] if i < 3 else proj_hidden[i - 3]
        pieces.append(jnp.dot(source, table, preferred_element_type=jnp.float32))
    columns = lax.psum(jnp.concatenate(pieces, axis=1), "tp")
    features = layer_features(columns, membership(row_count, seq_count))
    paired = lax.all_gather(queries, "sq", axis=1, tiled=True)
    return jnp.einsum("elk,lqk->eq", features, paired.astype(jnp.float32), precision=HIGH)


def solution(mesh):
    placed = (
        P(("groups", "sq"), "tp"),
        P(("groups", "sq"), "tp"),
        P("tp"),
        P("sq", "tp"),
        P("sq", "tp"),
        P("tp", "sq"),
        P(None, "tp", None),
        P(None, "tp", None),
        P(None, ("tp", "sq"), None),
    )
    body = ring_device if mesh.shape["tp"] == 8 else wide_device
    return jax.shard_map(
        body, mesh=mesh, in_specs=placed, out_specs=P(("groups", "sq"), "tp"), check_vma=False
    )
```

time: 446 us -> 157 us (0.35)
  waiting for transfers between devices: 337 us -> 0 us
  Pallas kernels: 0 us -> 149 us
  matrix products: 65.9 us -> 0 us
  blocking collectives: 19.2 us -> 0 us
  between operations: 13.6 us -> 0.01 us
  local copies, waits for them, and re-layouts: 2.52 us -> 7.02 us
    all_gather x5 -> x0, waiting for transfers between devices: 266 us -> none  [the longest x1 69.5 us: per_device(): shard_piece = lax.all_gather(normed, 'tp', axis=1, tiled=True)]
    pallas_call x0 -> x1, Pallas kernels: none -> 149 us  [ring_device(): pl.pallas_call(kernel, out_shape=jax.ShapeDtypeStruct((1, 32), f32), in_s...]
    psum x1 -> x0, waiting for transfers between devices: 68.9 us -> none  [per_device(): columns = lax.psum(jnp.concatenate(pieces, axis=1), 'tp')]
    dot_general x13 -> x0, matrix products: 65.9 us -> none  [the longest x1 20.7 us: per_device(): gate = jnp.dot(shard_piece, gate_full, preferred_element_type=jnp.float32)]
    psum x1 -> x0, blocking collectives: 16.8 us -> none  [per_device(): row_total = lax.psum(jnp.sum(states * states, axis=1), 'tp')]
  transfers between devices with their start and end apart: 6 -> 0, of which waited for: 6 -> 0; matrix products, arithmetic and copies ran while one was open for 9% -> 0% of each run, Pallas kernels for 0% -> 0%
where the time goes in v1:
time: 157 us; the launch traced here: 156 us
  Pallas kernels  149 us (95%)
  local copies, waits for them, and re-layouts  7.02 us (4%)
    pallas_call x1, Pallas kernels, ring_device(): pl.pallas_call(kernel, out_shape=jax.ShapeDtypeStruct((1, 32), f32), in_s...  149 us
    unnamed x3, local copies, waits for them, and re-layouts  5.74 us

profile of v1, /device:TPU:24, one launch (start us, length us, event | category | flops | bytes accessed | tf_op | source)
XLA Modules:
  0.0 156.4 jit_solution(8959050826914816283)
XLA Ops:
  0.0 1.3 reshape.3.gain_ref
  1.3 2.2 %copy.10.pm_ref = bf16[3,1024,64]{2,1,0:T(8,128)(2,1)} copy(bf16[3,1024,64]{1,2,0:T(8,128)(2,1)} %param.15) | data formatting | bytes 786432 | tf_op args[6]
  3.4 2.5 %copy.11.ph_ref = bf16[3,2048,64]{2,1,0:T(8,128)(2,1)} copy(bf16[3,2048,64]{1,2,0:T(8,128)(2,1)} %param.16) | data formatting | bytes 1572864 | tf_op args[7]
  5.9 149.3 %shard_map.91 = f32[1,32]{1,0:T(1,128)} custom-call(bf16[256,1024]{1,0:T(8,128)(2,1)} %hid_ref.1, bf16[256,1024]{1,0:T(8,128)(2,1)} %og_ref.1, bf16[1,1024]{1,0:T(2,128)(2,1)} %reshape.3.gain_ref, bf16[4096,2048]{1,0:T(8,128)(2,1)} %wg_ref.1, bf16[4096,2048]{1,0:T(8,128)(2,1)} %wu_ref.1, bf16[2048,4096]{1,0:T(8,128)(2,1)} %wd_ref.1, ...), custom_call_target="tpu_custom_call" | custom-call | flops 25999998976 | bytes 100000000 | tf_op jit(solution)/shard_map/pallas_call | solution.py:375
  155.2 1.1 copy.13

commit v2 on v1

--- a/solution.py
+++ b/solution.py
@@ -15,6 +15,10 @@
 NC = 4
 MESH = pl.DeviceIdType.MESH
 HIGH = lax.Precision.HIGHEST
+ORDER = tuple(sorted(((r, i) for r in range(2 * NB) for i in range(4)), key=lambda e: 7 * e[0] + 6 * e[1]))
+EARLY = 2
+FINISH_AFTER = ORDER[ORDER.index((2, 3)) + 1]
+USES = tuple(tuple(e for e in ORDER if e[0] // NB == a) for a in range(2))
 ARRIVALS = (
     (0, 2, 4, 6),
     (0, 1, 2, 4),
@@ -42,7 +46,7 @@
     o = 1 - s
     rows, width = hid.shape
     bt = rows // NB
-    hl = acc_a.shape[1]
+    hl = acc_a.shape[2]
     nc = hl // NC
     share = bt // 8
 
@@ -88,14 +92,15 @@
         ]
         steps.append((src_slot, target, passes))
 
-    def w_load(a, i):
+    def w_load(a, use):
+        i, slot_at = USES[a][use][1], use % 2
         at = steps[i][0] * width
         at = pl.multiple_of(at, width)
         if a == 0:
-            return [pltpu.make_async_copy(wd_ref.at[:, pl.ds(at, width)], wdb.at[i % 2], w_sem.at[0, i % 2])]
+            return [pltpu.make_async_copy(wd_ref.at[:, pl.ds(at, width)], wdb.at[slot_at], w_sem.at[0, slot_at])]
         return [
-            pltpu.make_async_copy(wg_ref.at[pl.ds(at, width), :], wgb.at[i % 2], w_sem.at[1, i % 2]),
-            pltpu.make_async_copy(wu_ref.at[pl.ds(at, width), :], wub.at[i % 2], w_sem.at[2, i % 2]),
+            pltpu.make_async_copy(wg_ref.at[pl.ds(at, width), :], wgb.at[slot_at], w_sem.at[1, slot_at]),
+            pltpu.make_async_copy(wu_ref.at[pl.ds(at, width), :], wub.at[slot_at], w_sem.at[2, slot_at]),
         ]
 
     for a in range(2):
@@ -136,7 +141,25 @@
         def _():
             here.start()
 
+    def relays(a, b, i, k):
+        src_slot, target, passes = steps[i]
+        chunk = grid_in.at[a, b, src_slot, k]
+        copy = remote(
+            chunk, chunk, relay_send.at[a, b, i, k], g_recv.at[a, b, src_slot, k], {"tp": target}
+        )
+        return copy, passes[k]
+
+    def arrive(a, b, i):
+        for k in range(2):
+            copy, passing = relays(a, b, i, k)
+            copy.wait_recv()
+
+            @pl.when(passing)
+            def _():
+                copy.start()
+
     own_start(0, 0)
+    own_start(0, 1)
     q_copy = remote(q_ref, qb.at[s], q_send, q_recv, {"sq": o})
     q_copy.start()
 
@@ -151,7 +174,9 @@
         c.start()
     loads[1].wait()
     loads[2].wait()
-    c2 = dot(og[...], pm[2])
+    c2 = dot(og[...], pm[2], ((1,), (1,)))
+    for r, i in ORDER[:EARLY]:
+        arrive(r // NB, r % NB, i)
     for c in rs_copies:
         c.wait_recv()
     total = rs[0]
@@ -161,51 +186,24 @@
     factor = jnp.transpose(jnp.broadcast_to(factor[0:1], (128, rows)))[:, 0:1]
     nm[...] = (hid[...].astype(jnp.float32) * factor * gain_ref[...].astype(jnp.float32)).astype(jnp.bfloat16)
     own_start(1, 0)
-    c0 = dot(nm[...], pm[0])
-    c1 = dot(nm[...], pm[1])
+    own_start(1, 1)
+    c0 = dot(nm[...], pm[0], ((1,), (1,)))
+    c1 = dot(nm[...], pm[1], ((1,), (1,)))
     for b in range(NB):
         part = slice(b * bt, (b + 1) * bt)
         cols[b, :, 0:128] = jnp.concatenate([c0[part], c1[part]], axis=1)
         cols[b, :, 128:256] = jnp.concatenate([c2[part], c2[part]], axis=1)
     loads[3].wait()
 
-    def relays(a, b, i, k):
-        src_slot, target, passes = steps[i]
-        chunk = grid_in.at[a, b, src_slot, k]
-        copy = remote(
-            chunk, chunk, relay_send.at[a, b, i, k], g_recv.at[a, b, src_slot, k], {"tp": target}
-        )
-        return copy, passes[k]
-
-    def arrive(a, b, i):
-        for k in range(2):
-            copy, passing = relays(a, b, i, k)
-            copy.wait_recv()
-
-            @pl.when(passing)
-            def _():
-                copy.start()
-
-    def refill(a, b, i):
-        if i < 2:
-            for c in w_load(a, i + 2):
-                c.start()
-        else:
-
-            @pl.when(b + 1 < NB)
-            def _():
-                for c in w_load(a, i - 2):
-                    c.start()
-
     def pa_copy(b):
         return remote(
-            acc_a.at[pl.ds(pl.multiple_of(o * bt, bt), bt), :], rec_a.at[b], pa_send.at[b], pa_recv.at[b], {"sq": o}
+            acc_a.at[b, pl.ds(pl.multiple_of(o * bt, bt), bt), :], rec_a.at[b], pa_send.at[b], pa_recv.at[b], {"sq": o}
         )
 
     def px_copy(b, n):
         lanes = pl.ds(pl.multiple_of(n * nc, nc), nc)
         return remote(
-            acc_gu.at[:, pl.ds(pl.multiple_of(o * bt, bt), bt), lanes],
+            acc_gu.at[b, :, pl.ds(pl.multiple_of(o * bt, bt), bt), lanes],
             rec_gu.at[b, :, :, lanes],
             px_send.at[b, n],
             px_recv.at[b, n],
@@ -222,69 +220,52 @@
             {"tp": peer},
         )
 
-    def block(b, carry):
-        @pl.when(b + 1 < NB)
-        def _():
-            own_start(0, b + 1)
-
-        for i in range(4):
-            arrive(0, b, i)
-            for c in w_load(0, i):
-                c.wait()
-            src_slot = steps[i][0]
-
-            def down(n, carry):
-                lanes = pl.ds(pl.multiple_of(n * nc, nc), nc)
-                lhs = grid_in[0, b, src_slot].reshape(2 * bt, width)
-                got = dot(lhs, wdb[i % 2, lanes, :], ((1,), (1,)))
-                acc_a[:, lanes] = got if i == 0 else acc_a[:, lanes] + got
+    def multiply(a, b, i):
+        use = USES[a].index((a * NB + b, i))
+        for c in w_load(a, use):
+            c.wait()
+        src_slot = steps[i][0]
+
+        def part(n, carry):
+            lanes = pl.ds(pl.multiple_of(n * nc, nc), nc)
+            lhs = grid_in[a, b, src_slot].reshape(2 * bt, width)
+            if a == 0:
+                got = dot(lhs, wdb[use % 2, lanes, :], ((1,), (1,)))
+                acc_a[b, :, lanes] = got if i == 0 else acc_a[b, :, lanes] + got
                 return carry
-
-            lax.fori_loop(0, NC, down, 0)
-            refill(0, b, i)
-        pa_copy(b).start()
-
-        @pl.when(b + 1 < NB)
-        def _():
-            own_start(1, b + 1)
-
-        for i in range(4):
-            arrive(1, b, i)
-            for c in w_load(1, i):
-                c.wait()
-            src_slot = steps[i][0]
-
-            def gate_up(n, carry):
-                lanes = pl.ds(pl.multiple_of(n * nc, nc), nc)
-                lhs = grid_in[1, b, src_slot].reshape(2 * bt, width)
-                for m, buf in ((0, wgb), (1, wub)):
-                    got = dot(lhs, buf[i % 2, :, lanes])
-                    acc_gu[m, :, lanes] = got if i == 0 else acc_gu[m, :, lanes] + got
-                if i == 3:
-                    px_copy(b, n).start()
-                return carry
-
-            lax.fori_loop(0, NC, gate_up, 0)
-            refill(1, b, i)
-
+            for m, buf in ((0, wgb), (1, wub)):
+                got = dot(lhs, buf[use % 2, :, lanes])
+                acc_gu[b, m, :, lanes] = got if i == 0 else acc_gu[b, m, :, lanes] + got
+            if i == 3:
+                px_copy(b, n).start()
+            return carry
+
+        lax.fori_loop(0, NC, part, 0)
+        if use + 2 < len(USES[a]):
+            for c in w_load(a, use + 2):
+                c.start()
+        if a == 0 and i == 3:
+            pa_copy(b).start()
+
+    def finish(b):
         pa_copy(b).wait_recv()
         mine = pl.ds(pl.multiple_of(s * bt, bt), bt)
 
         def hidden(n, carry):
             px_copy(b, n).wait_recv()
             lanes = pl.ds(pl.multiple_of(n * nc, nc), nc)
-            gate = acc_gu[0, mine, lanes] + rec_gu[b, 0, :, lanes]
-            upward = acc_gu[1, mine, lanes] + rec_gu[b, 1, :, lanes]
-            grad_act = acc_a[mine, lanes] + rec_a[b, :, lanes]
+            gate = acc_gu[b, 0, mine, lanes] + rec_gu[b, 0, :, lanes]
+            upward = acc_gu[b, 1, mine, lanes] + rec_gu[b, 1, :, lanes]
+            grad_act = acc_a[b, mine, lanes] + rec_a[b, :, lanes]
             sig = jax.nn.sigmoid(gate)
             swish = gate * sig
             activation = (swish * upward).astype(jnp.bfloat16)
             grad_gate = (grad_act * upward * sig * (1.0 + gate * (1.0 - sig))).astype(jnp.bfloat16)
             grad_up = (grad_act * swish).astype(jnp.bfloat16)
             return (
-                carry[0] + dot(grad_gate, ph[0, lanes, :]),
-                carry[1] + dot(grad_up, ph[1, lanes, :]),
-                carry[2] + dot(activation, ph[2, lanes, :]),
+                carry[0] + dot(grad_gate, ph[0, :, lanes], ((1,), (1,))),
+                carry[1] + dot(grad_up, ph[1, :, lanes], ((1,), (1,))),
+                carry[2] + dot(activation, ph[2, :, lanes], ((1,), (1,))),
             )
 
         zero = jnp.zeros((bt, R), jnp.float32)
@@ -293,12 +274,15 @@
         cols[b, :, 256:384] = jnp.concatenate([c4, c5], axis=1)
         for d in range(1, 8):
             c_copy(b, d).start()
-        pa_copy(b).wait_send()
-        for n in range(NC):
-            px_copy(b, n).wait_send()
-        return carry
-
-    lax.fori_loop(0, NB, block, 0)
+
+    for at, (r, i) in enumerate(ORDER):
+        if EARLY <= at + 1 < len(ORDER):
+            ahead, step = ORDER[at + 1]
+            arrive(ahead // NB, ahead % NB, step)
+        multiply(r // NB, r % NB, i)
+        if (r, i) == FINISH_AFTER:
+            finish(0)
+    finish(1)
 
     tokens = []
     for b in range(NB):
@@ -358,6 +342,9 @@
 
         for d in range(1, 8):
             c_copy(b, d).wait_send()
+        pa_copy(b).wait_send()
+        for n in range(NC):
+            px_copy(b, n).wait_send()
         return carry
 
     lax.fori_loop(0, NB, drain, 0)
@@ -381,16 +368,16 @@
             pltpu.VMEM((rows, width), bf),
             pltpu.VMEM((rows, width), bf),
             pltpu.VMEM((rows, width), bf),
-            pltpu.VMEM(proj_model.shape, bf),
-            pltpu.VMEM(proj_hidden.shape, bf),
+            pltpu.VMEM((3, R, width), bf),
+            pltpu.VMEM((3, R, hl), bf),
             pltpu.VMEM((2,) + queries.shape, bf),
             pltpu.VMEM((8, 8, rows), f32),
             pltpu.VMEM((2, NB, 4, 2, bt, width), bf),
             pltpu.VMEM((2, hl, width), bf),
             pltpu.VMEM((2, width, hl), bf),
             pltpu.VMEM((2, width, hl), bf),
-            pltpu.VMEM((2 * bt, hl), f32),
-            pltpu.VMEM((2, 2 * bt, hl), f32),
+            pltpu.VMEM((NB, 2 * bt, hl), f32),
+            pltpu.VMEM((NB, 2, 2 * bt, hl), f32),
             pltpu.VMEM((NB, bt, hl), f32),
             pltpu.VMEM((NB, 2, bt, hl), f32),
             pltpu.VMEM((NB, bt, 6 * R), f32),
@@ -421,7 +408,15 @@
         ),
         cost_estimate=pl.CostEstimate(flops=26 * 10**9, bytes_accessed=10**8, transcendentals=10**6),
     )(
-        hidden_states, out_grad, norm_gain.reshape(1, width), w_gate, w_up, w_down, proj_model, proj_hidden, queries
+        hidden_states,
+        out_grad,
+        norm_gain.reshape(1, width),
+        w_gate,
+        w_up,
+        w_down,
+        jnp.swapaxes(proj_model, 1, 2),
+        jnp.swapaxes(proj_hidden, 1, 2),
+        queries,
     )
 
 

time: 157 us -> 129 us (0.82)
  Pallas kernels: 149 us -> 127 us
  local copies, waits for them, and re-layouts: 7.02 us -> 2.39 us
    pallas_call x1, Pallas kernels: 149 us -> 127 us  [ring_device(): pl.pallas_call(kernel, out_shape=jax.ShapeDtypeStruct((1, 32), f32), in_s...]
    unnamed x3 -> x1, local copies, waits for them, and re-layouts: 5.74 us -> 1.11 us
where the time goes in v2:
time: 129 us
  Pallas kernels  127 us (98%)
  local copies, waits for them, and re-layouts  2.39 us (2%)
    pallas_call x1, Pallas kernels, ring_device(): pl.pallas_call(kernel, out_shape=jax.ShapeDtypeStruct((1, 32), f32), in_s...  127 us

profile of v2, /device:TPU:24, one launch (start us, length us, event | category | flops | bytes accessed | tf_op | source)
XLA Modules:
  0.0 129.0 jit_solution(1081088151939187167)
XLA Ops:
  0.0 1.3 reshape.3.gain_ref
  1.3 126.6 %shard_map.91 = f32[1,32]{1,0:T(1,128)} custom-call(bf16[256,1024]{1,0:T(8,128)(2,1)} %hid_ref.1, bf16[256,1024]{1,0:T(8,128)(2,1)} %og_ref.1, bf16[1,1024]{1,0:T(2,128)(2,1)} %reshape.3.gain_ref, bf16[4096,2048]{1,0:T(8,128)(2,1)} %wg_ref.1, bf16[4096,2048]{1,0:T(8,128)(2,1)} %wu_ref.1, bf16[2048,4096]{1,0:T(8,128)(2,1)} %wd_ref.1, ...), custom_call_target="tpu_custom_call" | custom-call | flops 25999998976 | bytes 100000000 | tf_op jit(solution)/shard_map/pallas_call | solution.py:362
  127.9 1.1 copy.11

commit v3 on v2

--- a/solution.py
+++ b/solution.py
@@ -276,9 +276,21 @@
             c_copy(b, d).start()
 
     for at, (r, i) in enumerate(ORDER):
-        if EARLY <= at + 1 < len(ORDER):
+        if EARLY <= at + 1 < len(ORDER) - 1:
             ahead, step = ORDER[at + 1]
             arrive(ahead // NB, ahead % NB, step)
+        if at == len(ORDER) - 2:
+
+            @pl.when(place < 4)
+            def _():
+                arrive(1, NB - 1, 3)
+
+        if at == len(ORDER) - 1:
+
+            @pl.when(place >= 4)
+            def _():
+                arrive(1, NB - 1, 3)
+
         multiply(r // NB, r % NB, i)
         if (r, i) == FINISH_AFTER:
             finish(0)

time: 129 us -> 127 us (0.984)
  Pallas kernels: 127 us -> 125 us
    pallas_call x1, Pallas kernels: 127 us -> 125 us  [ring_device(): pl.pallas_call(kernel, out_shape=jax.ShapeDtypeStruct((1, 32), f32), in_s...]
where the time goes in v3:
time: 127 us
  Pallas kernels  125 us (98%)
  local copies, waits for them, and re-layouts  2.39 us (2%)
    pallas_call x1, Pallas kernels, ring_device(): pl.pallas_call(kernel, out_shape=jax.ShapeDtypeStruct((1, 32), f32), in_s...  125 us

profile of v3, /device:TPU:24, one launch (start us, length us, event | category | flops | bytes accessed | tf_op | source)
XLA Modules:
  0.0 127.2 jit_solution(3198572470313824826)
XLA Ops:
  0.0 1.3 %reshape.3.gain_ref = bf16[1,1024]{1,0:T(2,128)(2,1)} reshape(bf16[1024]{0:T(1024)(128)(2,1)} %param.11) | data formatting | bytes 4096 | tf_op jit(solution)/shard_map/reshape | solution.py:425
  1.3 124.8 %shard_map.91 = f32[1,32]{1,0:T(1,128)} custom-call(bf16[256,1024]{1,0:T(8,128)(2,1)} %hid_ref.1, bf16[256,1024]{1,0:T(8,128)(2,1)} %og_ref.1, bf16[1,1024]{1,0:T(2,128)(2,1)} %reshape.3.gain_ref, bf16[4096,2048]{1,0:T(8,128)(2,1)} %wg_ref.1, bf16[4096,2048]{1,0:T(8,128)(2,1)} %wu_ref.1, bf16[2048,4096]{1,0:T(8,128)(2,1)} %wd_ref.1, ...), custom_call_target="tpu_custom_call" | custom-call | flops 25999998976 | bytes 100000000 | tf_op jit(solution)/shard_map/pallas_call | solution.py:374
  126.1 1.1 copy.11
